TPU v7x, 32 devices: a whole 2x2x4 slice. The times are simulated.
32 devices in a mesh: fsdp: 16 (over z, y, x), basis: 2 (over core).
Axes of the slice: x: 2, y: 2, z: 4, core: 2. Of those that a mesh axis runs over, the one named last changes fastest.
Arguments:
- gradient: bfloat16 [2, 576, 18432], P('basis', 'fsdp'), may hold values from -6000 to 6000
- first_moment: bfloat16 [2, 576, 18432], P('basis', 'fsdp'), may hold values from -0.29882812 to 0.29882812
- second_moment: bfloat16 [2, 576, 18432], P('basis', None, 'fsdp'), may hold values from 0.0099487305 to 0.5
- statistic: float32 [2, 576, 576], P('basis', 'fsdp'), may hold values from -1 to 3, as said below
- eigenbasis: float32 [2, 576, 576], P('basis', 'fsdp'), may hold values from -1 to 2, as said below
Outputs:
- update: bfloat16 [2, 576, 18432], P('basis', 'fsdp')
- new_first: bfloat16 [2, 576, 18432], P('basis', 'fsdp')
- new_second: bfloat16 [2, 576, 18432], P('basis', None, 'fsdp')
- new_stat: float32 [2, 576, 576], P('basis', 'fsdp')
- new_basis: float32 [2, 576, 576], P('basis', 'fsdp')
Inputs may be any that keep to these rules, and one draw needn't show every extreme that they name: `statistic`: symmetric in each block, positive definite. `eigenbasis`: each block invertible.
All inputs are finite; a program needn't handle non-finite values.
Results may differ from a plain program's by a relative error of at most 0.00055.
The roundings to bfloat16 on the way count: a program that leaves them out, or rounds other values in their place, can miss the bound.
Values may be sent and summed in bfloat16 or wider, within the bound.
A program may use at most 128 MiB of HBM per device.

v0:
```python
import jax
import jax.numpy as jnp
from jax import lax
from jax.sharding import PartitionSpec as P

FF = 18432


beta_first = 0.9
beta_second = 0.95
clip_rms = 0.5
tiny_eps = 1e-08


def lead_dot(left, right, precision_mode):
    return lax.dot_general(
        left,
        right,
        (((0,), (0,)), ((), ())),
        preferred_element_type=jnp.float32,
        precision=precision_mode,
    )


def local(gradient, first_moment, second_moment, statistic, eigenbasis):
    entries = gradient.shape[1] * gradient.shape[2] * lax.axis_size("fsdp") * lax.axis_size("basis")
    local_squares = jnp.sum(jnp.square(gradient.astype(jnp.float32)))
    total_squares = lax.psum(local_squares, ("fsdp", "basis"))
    clip_factor = jnp.minimum(1.0, clip_rms / jnp.sqrt(total_squares / entries + 1e-06))
    new_first = (
        beta_first * first_moment.astype(jnp.float32)
        + (1.0 - beta_first) * clip_factor * gradient.astype(jnp.float32)
    ).astype(jnp.bfloat16)
    grad_cols, moment_cols = (
        lax.all_to_all(gradient, "fsdp", split_axis=2, concat_axis=1, tiled=True),
        lax.all_to_all(first_moment, "fsdp", split_axis=2, concat_axis=1, tiled=True),
    )
    full_basis = lax.all_gather(eigenbasis, "fsdp", axis=1, tiled=True)[0]
    rounded_basis = full_basis.astype(jnp.bfloat16)
    block_cols = grad_cols[0]
    grad_rot = lead_dot(rounded_basis, block_cols, None)
    moment_rot = lead_dot(rounded_basis, moment_cols[0], None)
    scaled_rot = clip_factor * grad_rot
    rotated_first = beta_first * moment_rot + (1.0 - beta_first) * scaled_rot
    second_full = (
        beta_second * second_moment[0].astype(jnp.float32)
        + (1.0 - beta_second) * scaled_rot * scaled_rot
    )
    direction = (rotated_first / (jnp.sqrt(second_full) + tiny_eps)).astype(jnp.bfloat16)
    update_cols = jnp.dot(rounded_basis, direction, preferred_element_type=jnp.float32).astype(
        jnp.bfloat16
    )
    update = lax.all_to_all(update_cols[None], "fsdp", split_axis=1, concat_axis=2, tiled=True)
    stat_share = lax.psum_scatter(
        lax.dot_general(
            block_cols, block_cols, (((1,), (1,)), ((), ())), preferred_element_type=jnp.float32
        )
        / FF,
        "fsdp",
        scatter_dimension=0,
        tiled=True,
    )
    new_stat = (
        beta_second * statistic[0] + (1.0 - beta_second) * clip_factor * clip_factor * stat_share
    )
    refreshed = jnp.dot(new_stat, full_basis, precision=lax.Precision.HIGHEST)
    gram_matrix = lax.psum(lead_dot(refreshed, refreshed, lax.Precision.HIGHEST), "fsdp")
    factor = jnp.linalg.cholesky(gram_matrix)
    new_basis = lax.linalg.triangular_solve(
        factor, refreshed, left_side=False, lower=True, transpose_a=True
    )
    return (
        update,
        new_first,
        second_full.astype(jnp.bfloat16)[None],
        new_stat[None],
        new_basis[None],
    )


def solution(mesh):
    return jax.shard_map(
        local,
        mesh=mesh,
        in_specs=(
            P("basis", "fsdp", None),
            P("basis", "fsdp", None),
            P("basis", None, "fsdp"),
            P("basis", "fsdp", None),
            P("basis", "fsdp", None),
        ),
        out_specs=(
            P("basis", "fsdp", None),
            P("basis", "fsdp", None),
            P("basis", None, "fsdp"),
            P("basis", "fsdp", None),
            P("basis", "fsdp", None),
        ),
        check_vma=False,
    )
```

profile of v0, /device:TPU:26, one launch (start us, length us, event | category | flops | bytes accessed | tf_op | source)
XLA Modules:
  0.0 814.6 jit_solution(18049985885864724341)
XLA Ops:
  7.2 18.2 %copy.46 = bf16[1,36,18432]{1,0,2:T(2,128)(2,1)} copy(bf16[1,36,18432]{2,1,0:T(8,128)(2,1)} %param.5) | data formatting | bytes 2654208 | tf_op args[0]
  25.9 101.9 %reduce.33 = bf16[18432,36]{1,0:T(8,128)(2,1)} reduce(bf16[18432,1,36]{2,1,0:T(2,128)(2,1)} %bitcast.138, bf16[]{:T(256)} %broadcast.253), dimensions={1}, to_apply=%bitcast.103.reduce_sub_computation | reduce | bytes 2654210
  127.8 12.9 %reshape.88 = bf16[16,2,20736]{2,1,0:T(2,128)(2,1)} reshape(bf16[18432,36]{1,0:T(8,128)(2,1)} %reduce.33) | data formatting | bytes 2654208
  140.7 7.2 all-to-all-start.1
  150.6 14.6 %copy.43 = bf16[1,36,18432]{1,0,2:T(2,128)(2,1)} copy(bf16[1,36,18432]{2,1,0:T(8,128)(2,1)S(1)} %copy-done.1) | data formatting | bytes 2654208 | tf_op args[1]
  165.2 101.9 %reduce.32 = bf16[18432,36]{1,0:T(8,128)(2,1)} reduce(bf16[18432,1,36]{2,1,0:T(2,128)(2,1)} %bitcast.141, bf16[]{:T(256)} %broadcast.253), dimensions={1}, to_apply=%bitcast.101.reduce_sub_computation | reduce | bytes 2654210
  267.1 12.9 %reshape.86 = bf16[16,2,20736]{2,1,0:T(2,128)(2,1)} reshape(bf16[18432,36]{1,0:T(8,128)(2,1)} %reduce.32) | data formatting | bytes 2654208
  280.0 40.2 %psum.14 = f32[]{:T(128)} all-reduce(f32[]{:T(128)} %fusion.4), channel_id=1, replica_groups=mesh['fsdp'=16,'basis'=2] {'fsdp','basis'}, use_global_device_ids=true, to_apply=%region_1.0 | all-reduce | flops 1 | bytes 8 | tf_op jit(solution)/shard_map/psum | solution.py:28
  322.7 1.6 fusion.6
  324.4 6.3 all-to-all-start
  330.7 12.6 %all-reduce.7.cloned.1.call-start = ((), (), s32[]{:S(2)}) async-start(), calls=%async_computation.4 | async-start | bytes 2949120 | tf_op jit(solution)/shard_map/psum | solution.py:67
  343.3 16.5 %reshape.89 = bf16[18432,1,36]{2,1,0:T(2,128)(2,1)} reshape(bf16[16,2,20736]{2,1,0:T(2,128)(2,1)} %all-to-all-done.1) | data formatting | bytes 2654208
  359.8 18.0 %copy.47 = bf16[1,36,18432]{2,1,0:T(8,128)(2,1)S(1)} copy(bf16[1,36,18432]{1,0,2:T(2,128)(2,1)} %bitcast.139) | data formatting | bytes 2654208 | tf_op jit(solution)/shard_map/all_to_all | solution.py:35
  379.5 3.1 convolution_multiply_fusion.2
  382.7 49.6 %fusion = f32[48,576]{1,0:T(8,128)S(1)} fusion(f32[576,576]{1,0:T(8,128)S(1)} %convolution_multiply_fusion.2), kind=kCustom, calls=%all-reduce-scatter | all-reduce-scatter fusion | flops 442369 | bytes 1438208
  434.2 2.2 collective-permute-start.1
  436.4 2.1 collective-permute-start
  438.6 14.7 %reshape.87 = bf16[18432,1,36]{2,1,0:T(2,128)(2,1)} reshape(bf16[16,2,20736]{2,1,0:T(2,128)(2,1)S(1)} %all-to-all-done) | data formatting | bytes 2654208
  453.3 18.0 %copy.44 = bf16[1,36,18432]{2,1,0:T(8,128)(2,1)S(1)} copy(bf16[1,36,18432]{1,0,2:T(2,128)(2,1)} %bitcast.140) | data formatting | bytes 2654208 | tf_op jit(solution)/shard_map/all_to_all | solution.py:36
  471.5 1.4 collective-permute-start.3
  473.1 4.2 convolution_multiply_fusion
  478.7 2.4 collective-permute-done.3
  481.1 3.1 concatenate.16
  486.0 2.5 fusion.73
  488.6 6.8 fusion.7
  495.3 3.4 copy.80
  498.7 10.2 %reduce.34 = bf16[576,1152]{1,0:T(8,128)(2,1)} reduce(bf16[576,1,1152]{2,1,0:T(2,128)(2,1)S(1)} %bitcast.142, bf16[]{:T(256)} %broadcast.253), dimensions={1}, to_apply=%bitcast.131.reduce_sub_computation | reduce | bytes 2654210
  508.9 4.0 reshape.90
  512.9 10.3 %all-to-all-start.2 = ((bf16[16,2,20736]{2,1,0:T(2,128)(2,1)}), bf16[16,2,20736]{2,1,0:T(2,128)(2,1)}, u32[]{:S(2)}, u32[]{:S(2)}) async-start(bf16[16,2,20736]{2,1,0:T(2,128)(2,1)} %reshape.90), calls=%async_computation.2 | async-start | bytes 2654208 | tf_op jit(solution)/shard_map/all_to_all | solution.py:53
  523.3 2.9 fusion.13
  527.8 86.9 %all-reduce.7.cloned.1.call-done = f32[576,576]{0,1:T(8,128)} async-done(((f32[576,576]{0,1:T(8,128)}), f32[576,576]{0,1:T(8,128)}) %all-reduce.7.cloned.1.call-update) | async-done | bytes 1327120 | tf_op jit(solution)/shard_map/psum | solution.py:67
  614.7 2.0 copy.53
  617.9 11.7 %cholesky.134 = f32[128,128]{1,0:T(8,128)S(1)} custom-call(f32[128,128]{1,0:T(8,128)S(1)} %cholesky.346), custom_call_target="Cholesky" | custom-call | tf_op jit(solution)/shard_map/jit(cholesky)/cholesky | solution.py:68
  629.8 9.8 %custom-call.38 = f32[1,128,128]{1,2,0:T(8,128)S(1)} custom-call(f32[1,128,128]{2,1,0:T(8,128)S(1)} %get-tuple-element.58), custom_call_target="InvertDiagBlocksLowerTriangular" | custom-call | tf_op jit(solution)/shard_map/jit(cholesky)/cholesky | solution.py:68
  641.0 13.2 %cholesky.274 = f32[128,128]{1,0:T(8,128)} custom-call(f32[128,128]{1,0:T(8,128)} %cholesky.350), custom_call_target="Cholesky" | custom-call | tf_op jit(solution)/shard_map/jit(cholesky)/cholesky | solution.py:68
  654.1 1.5 select_reduce_fusion.2
  655.6 11.4 %custom-call.39 = f32[1,128,128]{1,2,0:T(8,128)} custom-call(f32[1,128,128]{2,1,0:T(8,128)} %get-tuple-element.55), custom_call_target="InvertDiagBlocksLowerTriangular" | custom-call | tf_op jit(solution)/shard_map/jit(cholesky)/cholesky | solution.py:68
  669.2 12.5 %cholesky.295 = f32[128,128]{1,0:T(8,128)S(1)} custom-call(f32[128,128]{1,0:T(8,128)} %cholesky.355), custom_call_target="Cholesky" | custom-call | tf_op jit(solution)/shard_map/jit(cholesky)/cholesky | solution.py:68
  682.4 10.6 %custom-call.40 = f32[1,128,128]{1,2,0:T(8,128)S(1)} custom-call(f32[1,128,128]{2,1,0:T(8,128)} %get-tuple-element.52), custom_call_target="InvertDiagBlocksLowerTriangular" | custom-call | tf_op jit(solution)/shard_map/jit(cholesky)/cholesky | solution.py:68
  693.8 11.9 %cholesky.314 = f32[128,128]{1,0:T(8,128)S(1)} custom-call(f32[128,128]{1,0:T(8,128)S(1)} %cholesky.360), custom_call_target="Cholesky" | custom-call | tf_op jit(solution)/shard_map/jit(cholesky)/cholesky | solution.py:68
  706.2 9.8 %custom-call.41 = f32[1,128,128]{1,2,0:T(8,128)S(1)} custom-call(f32[1,128,128]{2,1,0:T(8,128)S(1)} %get-tuple-element.49), custom_call_target="InvertDiagBlocksLowerTriangular" | custom-call | tf_op jit(solution)/shard_map/jit(cholesky)/cholesky | solution.py:68
  716.5 5.8 cholesky.334
  729.6 8.0 while.1
  737.7 49.1 %custom-call.42 = f32[5,128,128]{1,2,0:T(8,128)S(1)} custom-call(f32[5,128,128]{2,1,0:T(8,128)S(1)} %pad_maximum_fusion), custom_call_target="InvertDiagBlocksLowerTriangular" | custom-call | tf_op jit(solution)/shard_map/triangular_solve | solution.py:69
  789.7 4.6 reshape.91
  794.3 8.8 %bitcast_reduce_fusion = bf16[576,1152]{1,0:T(8,128)(2,1)} fusion(bf16[576,1,1152]{2,1,0:T(2,128)(2,1)S(1)} %reshape.91), kind=kLoop, calls=%fused_computation.135 | loop fusion | bytes 2654208 | tf_op jit(solution)/shard_map/all_to_all | solution.py:53
  803.1 2.2 all_to_all.42
  805.5 1.8 all_to_all.44
  (108 shorter events, 35.4 us)
Async XLA Ops:
  140.7 8.0 copy-start
  140.7 9.9 %copy-start.1 = (bf16[1,36,18432]{2,1,0:T(8,128)(2,1)S(1)}, bf16[1,36,18432]{2,1,0:T(8,128)(2,1)}, u32[]{:S(2)}) copy-start(bf16[1,36,18432]{2,1,0:T(8,128)(2,1)} %param.6) | copy-start | bytes 3981316
  140.7 183.7 %all-to-all-start.1 = ((bf16[16,2,20736]{2,1,0:T(2,128)(2,1)}), bf16[16,2,20736]{2,1,0:T(2,128)(2,1)}, u32[]{:S(2)}, u32[]{:S(2)}) async-start(bf16[16,2,20736]{2,1,0:T(2,128)(2,1)} %reshape.88), calls=%async_computation.1 | async-start | bytes 2654208 | tf_op jit(solution)/shard_map/all_to_all | solution.py:35
  147.9 325.1 %all-gather.2.cloned.1.call-start = ((), (), s32[]{:S(2)}) async-start(), calls=%async_computation.3 | async-start | bytes 1566720 | tf_op jit(solution)/shard_map/all_gather | solution.py:38
  267.1 54.4 %copy-start.12 = (u32[32]{0:T(128)S(1)}, u32[32]{0:T(128)}, u32[]{:S(2)}) copy-start(u32[32]{0:T(128)} %constant.234) | copy-start | bytes 388
  324.4 114.2 %all-to-all-start = ((bf16[16,2,20736]{2,1,0:T(2,128)(2,1)}), bf16[16,2,20736]{2,1,0:T(2,128)(2,1)S(1)}, u32[]{:S(2)}, u32[]{:S(2)}) async-start(bf16[16,2,20736]{2,1,0:T(2,128)(2,1)} %reshape.86), calls=%async_computation | async-start | bytes 2654208 | tf_op jit(solution)/shard_map/all_to_all | solution.py:36
  330.7 284.0 %all-reduce.7.cloned.1.call-start = ((), (), s32[]{:S(2)}) async-start(), calls=%async_computation.4 | async-start | bytes 2949120 | tf_op jit(solution)/shard_map/psum | solution.py:67
  432.9 48.2 %collective-permute-start.2 = (f32[48,576]{1,0:T(8,128)S(1)}, f32[48,576]{1,0:T(8,128)}, u32[]{:S(2)}, u32[]{:S(2)}) collective-permute-start(f32[48,576]{1,0:T(8,128)S(1)} %fusion), channel_id=1, source_target_pairs={{0,6},{2,8},{4,10},{6,12},{8,14},{10,16},{12,18},{14,20},{16,22},{... | collective-permute-start | bytes 331784
  434.2 47.0 %collective-permute-start.1 = (f32[48,576]{1,0:T(8,128)S(1)}, f32[48,576]{1,0:T(8,128)}, u32[]{:S(2)}, u32[]{:S(2)}) collective-permute-start(f32[48,576]{1,0:T(8,128)S(1)} %fusion), channel_id=1, source_target_pairs={{0,4},{2,6},{4,8},{6,10},{8,12},{10,14},{12,16},{14,18},{16,20},{1... | collective-permute-start | bytes 331784
  436.4 44.7 %collective-permute-start = (f32[48,576]{1,0:T(8,128)S(1)}, f32[48,576]{1,0:T(8,128)}, u32[]{:S(2)}, u32[]{:S(2)}) collective-permute-start(f32[48,576]{1,0:T(8,128)S(1)} %fusion), channel_id=1, source_target_pairs={{0,2},{2,4},{4,6},{6,8},{8,10},{10,12},{12,14},{14,16},{16,18},{18... | collective-permute-start | bytes 331784
  471.5 1.6 copy-start.8
  471.5 9.7 %collective-permute-start.3 = (f32[36,576]{1,0:T(8,128)}, f32[36,576]{1,0:T(8,128)S(1)}, u32[]{:S(2)}, u32[]{:S(2)}) collective-permute-start(f32[36,576]{1,0:T(8,128)} %slice.146), channel_id=1, source_target_pairs={{0,8},{2,10},{4,12},{6,14},{8,16},{10,18},{12,20},{14,22},{16,24},... | collective-permute-start | bytes 248840
  477.5 7.6 copy-start.7
  477.5 7.6 copy-start.10
  484.3 0.8 copy-start.9
  486.0 2.5 copy-start.5
  512.9 10.3 %copy-start.6 = (f32[576,1152]{1,0:T(8,128)S(1)}, f32[576,1152]{1,0:T(8,128)}, u32[]{:S(2)}) copy-start(f32[576,1152]{1,0:T(8,128)} %convolution_multiply_fusion) | copy-start | bytes 7962628
  512.9 276.8 %all-to-all-start.2 = ((bf16[16,2,20736]{2,1,0:T(2,128)(2,1)}), bf16[16,2,20736]{2,1,0:T(2,128)(2,1)}, u32[]{:S(2)}, u32[]{:S(2)}) async-start(bf16[16,2,20736]{2,1,0:T(2,128)(2,1)} %reshape.90), calls=%async_computation.2 | async-start | bytes 2654208 | tf_op jit(solution)/shard_map/all_to_all | solution.py:53
  614.7 2.0 copy-start.2
  616.8 1.1 copy-start.3
  617.9 21.7 %copy-start.4 = (f32[576,576]{1,0:T(8,128)S(1)}, f32[576,576]{1,0:T(8,128)}, u32[]{:S(2)}) copy-start(f32[576,576]{1,0:T(8,128)} %copy-done.3) | copy-start | bytes 3981316
  728.9 0.7 copy-start.13
  729.0 8.7 %copy-start.11 = (f32[128,64]{1,0:T(8,128)S(1)}, f32[128,64]{1,0:T(8,128)}, u32[]{:S(2)}) copy-start(f32[128,64]{1,0:T(8,128)} %pad_convert_fusion) | copy-start | bytes 98308
Sparse Core Ops, SparseCore 0:
  151.4 61.8 all-gather.1
  488.7 125.9 all-reduce.6
where the time goes:
time: 829 us; the launch traced here: 815 us
  other arithmetic  374 us (45%)
  local copies, waits for them, and re-layouts  174 us (21%)
  waiting for transfers between devices  89.8 us (11%)
  blocking collectives  89.7 us (11%)
  starting transfers between devices  43.9 us (5%)
  matrix products  22.9 us (3%)
  between operations  19.6 us (2%)
    unnamed x4, other arithmetic  214 us
    unnamed x44, local copies, waits for them, and re-layouts  108 us
    another operation x18, other arithmetic, local(): factor = jnp.linalg.cholesky(gram_matrix)  103 us
    psum x1, waiting for transfers between devices, local(): lax.psum(lead_dot(refreshed, refreshed, lax.Precision.HIGHEST), 'fsdp')  86.9 us
    another operation x7, other arithmetic, local(): lax.linalg.triangular_solve(factor, refreshed, left_side=False, lower=Tru...  50.6 us
    unnamed x1, blocking collectives  49.6 us
    psum x1, blocking collectives, local(): total_squares = lax.psum(local_squares, ('fsdp', 'basis'))  40.2 us
    all_to_all x3, local copies, waits for them, and re-layouts, local(): lax.all_to_all(gradient, 'fsdp', split_axis=2, concat_axis=1, tiled=True)  18.3 us
  transfers between devices with their start and end apart: 9, of which 2 were waited for; matrix products, arithmetic and copies ran while one was open for 57% of the time, Pallas kernels for 0%

commit v1 on v0

v1 whole, which is shorter than its diff:
```python
import functools

import jax
import jax.numpy as jnp
import numpy as np
from jax import lax
from jax.experimental import pallas as pl
from jax.experimental.pallas import tpu as pltpu
from jax.sharding import PartitionSpec as P

beta_first = 0.9
beta_second = 0.95
clip_rms = 0.5
tiny_eps = 1e-08
NB = 128
MESH = pl.DeviceIdType.MESH
HI = lax.Precision.HIGHEST
F32 = jnp.float32
BF16 = jnp.bfloat16


def dot(left, right, dims, precision=None):
    return lax.dot_general(
        left, right, (dims, ((), ())), preferred_element_type=F32, precision=precision
    )


def inverse_factor(tiles):
    lane = lax.broadcasted_iota(jnp.int32, (8, NB), 1)
    row = lax.broadcasted_iota(jnp.int32, (8, NB), 0)
    count = NB // 8
    for j in range(NB):
        home, sub = divmod(j, 8)
        pivot_row = tiles[home][sub : sub + 1, :]
        inverse = 1.0 / pivot_row[:, j : j + 1]
        at_j = lane == j
        scaled = jnp.where(at_j[:1], 1.0, pivot_row) * inverse
        for t in range(home, count):
            column = tiles[t][:, j : j + 1]
            updated = jnp.where(at_j, 0.0, tiles[t]) - column * scaled
            tiles[t] = jnp.where(row > sub, updated, tiles[t]) if t == home else updated
    out = []
    for t in range(count):
        on_diag = lane == row + 8 * t
        pivot = jnp.sum(jnp.where(on_diag, tiles[t], 0.0), axis=1, keepdims=True)
        unit = jnp.where(on_diag, 1.0, jnp.where(lane < row + 8 * t, tiles[t], 0.0))
        out.append(unit * lax.rsqrt(pivot))
    return jnp.concatenate(out, axis=0)


def kernel(
    n, nb, entries, cols, bk, split,
    g_ref, m_ref, v_ref, st_ref, eb_ref, pm_ref,
    upd_ref, nf_ref, ns_ref, nst_ref, q_ref,
    gs, ms, us, gr, bs, bb, covs, rs, ss, gc, rf, af, ro, sums_a, sums_b, lin,
    g_s, g_r, m_s, m_r, u_s, u_r, b_s, b_r, c_s, c_r, a_s, a_r, x_s, x_r, y_s, y_r, own_sem,
):
    me = lax.axis_index("fsdp")
    core = lax.axis_index("basis")
    rp = gs.shape[1]
    rf_rows = bs.shape[1]
    kp = bs.shape[2]
    total = n * cols
    width = 384 if cols % 384 == 0 else cols
    fold = 8 * 128

    def chunk(ref, d):
        if split:
            return ref.at[d]
        return ref.at[:, pl.ds(pl.multiple_of(d * cols, 128), cols)]

    def peers(fn):
        def body(k, carry):
            fn(lax.rem(me + k, n))
            return carry
        lax.fori_loop(1, n, body, 0)

    def send(source_of, target, s_sem, r_sem):
        def one(d):
            pltpu.make_async_remote_copy(
                src_ref=source_of(d), dst_ref=target(me), send_sem=s_sem.at[d],
                recv_sem=r_sem.at[me], device_id={"fsdp": d}, device_id_type=MESH,
            ).start()
        peers(one)

    def wait_recv(source_of, target, s_sem, r_sem):
        def one(d):
            pltpu.make_async_remote_copy(
                src_ref=source_of(d), dst_ref=target(d), send_sem=s_sem.at[d],
                recv_sem=r_sem.at[d], device_id={"fsdp": d}, device_id_type=MESH,
            ).wait_recv()
        peers(one)

    def wait_send(source_of, target, s_sem, r_sem):
        def one(d):
            pltpu.make_async_remote_copy(
                src_ref=source_of(d), dst_ref=target(me), send_sem=s_sem.at[d],
                recv_sem=r_sem.at[me], device_id={"fsdp": d}, device_id_type=MESH,
            ).wait_send()
        peers(one)

    grads = (lambda d: chunk(g_ref, d), lambda s: gs.at[s], g_s, g_r)
    moments = (lambda d: chunk(m_ref, d), lambda s: ms.at[s], m_s, m_r)
    updates = (lambda d: us.at[d], lambda s: chunk(upd_ref, s), u_s, u_r)
    bases = (lambda d: eb_ref, lambda s: bs.at[s], b_s, b_r)
    shares = (lambda d: covs.at[d], lambda s: rs.at[s], c_s, c_r)
    stats = (lambda d: nst_ref, lambda s: ss.at[s], a_s, a_r)
    squares = (lambda d: sums_a.at[n], lambda s: sums_a.at[s], x_s, x_r)

    barrier = pltpu.get_barrier_semaphore()

    def greet(d):
        pl.semaphore_signal(barrier, inc=1, device_id={"fsdp": d}, device_id_type=MESH)

    peers(greet)
    for k in range(1, nb):
        pl.semaphore_signal(
            barrier, inc=1, device_id={"basis": lax.rem(core + k, nb)}, device_id_type=MESH
        )
    pl.semaphore_wait(barrier, n - 1 + nb - 1)

    send(*grads)
    send(*bases)
    own = [
        pltpu.make_async_copy(chunk(g_ref, me), gs.at[me], own_sem.at[0]),
        pltpu.make_async_copy(chunk(m_ref, me), ms.at[me], own_sem.at[1]),
        pltpu.make_async_copy(eb_ref, bs.at[me], own_sem.at[2]),
    ]
    for copy in own:
        copy.start()

    def add_squares(d, acc):
        v = chunk(g_ref, d)[...].astype(F32)
        return acc + jnp.sum(v * v, axis=0, keepdims=True)

    acc = lax.fori_loop(0, n, add_squares, jnp.zeros((1, cols), F32))
    sums_a[n] = jnp.full((8, 128), jnp.sum(acc), F32)
    send(*squares)
    sums_a[me] = sums_a[n]
    wait_recv(*squares)
    sums_b[nb] = jnp.sum(sums_a[0:n], axis=0)
    sums_b[core] = sums_b[nb]

    def cross(k):
        other = lax.rem(core + k, nb)
        return pltpu.make_async_remote_copy(
            src_ref=sums_b.at[nb], dst_ref=sums_b.at[core], send_sem=y_s.at[other],
            recv_sem=y_r.at[core], device_id={"basis": other}, device_id_type=MESH,
        )

    def cross_recv(k):
        other = lax.rem(core + k, nb)
        return pltpu.make_async_remote_copy(
            src_ref=sums_b.at[nb], dst_ref=sums_b.at[other], send_sem=y_s.at[other],
            recv_sem=y_r.at[other], device_id={"basis": other}, device_id_type=MESH,
        )

    for k in range(1, nb):
        cross(k).start()

    for copy in own:
        copy.wait()
    wait_recv(*grads)
    gc[...] = dot(pm_ref[...], gs[...].reshape(n * rp, cols), ((1,), (0,))).astype(BF16)

    def share(s, carry):
        covs[s] = dot(gs[s], gc[...], ((1,), (1,)))[:rf_rows]
        return carry

    lax.fori_loop(0, n, share, 0)
    send(*shares)

    for k in range(1, nb):
        cross_recv(k).wait_recv()
    mean = jnp.sum(sums_b[0:nb], axis=0)[0:1, 0:1] / entries
    clip = jnp.minimum(1.0, clip_rms / jnp.sqrt(mean + 1e-06))

    def first(d, carry):
        chunk(nf_ref, d)[...] = (
            beta_first * chunk(m_ref, d)[...].astype(F32)
            + (1.0 - beta_first) * clip * chunk(g_ref, d)[...].astype(F32)
        ).astype(BF16)
        return carry

    lax.fori_loop(0, n, first, 0)

    wait_recv(*bases)

    def narrow(s, carry):
        v = bs[s]
        if rp > rf_rows:
            v = jnp.concatenate([v, jnp.zeros((rp - rf_rows, kp), F32)], axis=0)
        bb[s] = v.astype(BF16)
        return carry

    lax.fori_loop(0, n, narrow, 0)

    def columns(i):
        if cols == width:
            return pl.ds(0, cols)
        return pl.ds(pl.multiple_of(i * width, 128), width)

    def rotate(i, carry):
        at = columns(i)
        basis = bb[...].reshape(n * rp, kp)[:, :bk]
        rot = clip * dot(basis, gs[:, :, at].reshape(n * rp, width), ((0,), (0,)))
        gr[:, at] = rot
        ns_ref[:, at] = (
            beta_second * v_ref[:, at].astype(F32) + (1.0 - beta_second) * rot * rot
        ).astype(BF16)
        return carry

    lax.fori_loop(0, cols // width, rotate, 0)

    wait_recv(*shares)
    rs[me] = covs[me]

    def add_share(s, acc):
        return acc + rs[s]

    cov = lax.fori_loop(0, n, add_share, jnp.zeros((rf_rows, kp), F32)) / total
    nst_ref[...] = beta_second * st_ref[...] + (1.0 - beta_second) * clip * clip * cov
    send(*stats)
    send(*moments)
    ss[me] = nst_ref[...]
    wait_recv(*stats)

    def refresh(i, carry):
        at = pl.ds(pl.multiple_of(i * NB, NB), NB)
        rf[at, :] = dot(
            ss[:, :, at].reshape(n * rf_rows, NB), bs[...].reshape(n * rf_rows, kp),
            ((0,), (0,)), HI,
        )
        return carry

    lax.fori_loop(0, kp // NB, refresh, 0)
    rows = bk // n
    r_at = lax.broadcasted_iota(jnp.int32, (rf_rows, kp), 0)
    c_at = lax.broadcasted_iota(jnp.int32, (rf_rows, kp), 1)
    pick = jnp.where((c_at == r_at + me * rows) & (r_at < rows), 1.0, 0.0).astype(F32)
    ro[...] = dot(pick, rf[...], ((1,), (0,)), HI)

    def gram(i, carry):
        at = pl.ds(pl.multiple_of(i * NB, NB), NB)
        part = dot(rf[:, at], rf[...], ((0,), (0,)), HI)
        r = lax.broadcasted_iota(jnp.int32, (NB, kp), 0) + i * NB
        c = lax.broadcasted_iota(jnp.int32, (NB, kp), 1)
        af[at, :] = part + jnp.where((r == c) & (r >= bk), 1.0, 0.0)
        return carry

    lax.fori_loop(0, kp // NB, gram, 0)

    def precondition():
        wait_recv(*moments)

        def body(i, carry):
            at = columns(i)
            basis = bb[...].reshape(n * rp, kp)[:, :bk]
            rot = gr[:, at]
            moment = dot(basis, ms[:, :, at].reshape(n * rp, width), ((0,), (0,)))
            second = beta_second * v_ref[:, at].astype(F32) + (1.0 - beta_second) * rot * rot
            direction = (
                (beta_first * moment + (1.0 - beta_first) * rot) / (jnp.sqrt(second) + tiny_eps)
            ).astype(BF16)
            us[:, :, at] = (
                dot(basis, direction, ((1,), (0,))).astype(BF16).reshape(n, rp, width)
            )
            return carry

        lax.fori_loop(0, cols // width, body, 0)
        send(*updates)
        chunk(upd_ref, me)[...] = us[me]

    blocks = kp // NB

    def eliminate(b, carry):
        @pl.when(b == blocks // 2)
        def _():
            precondition()

        at = pl.ds(pl.multiple_of(b * NB, NB), NB)
        tiles = [
            af[pl.ds(pl.multiple_of(b * NB + 8 * t, 8), 8), at] for t in range(NB // 8)
        ]
        lin[...] = inverse_factor(tiles)
        panel = dot(lin[...], af[at, :], ((1,), (0,)), HI)
        q = dot(ro[:, at], lin[...], ((1,), (1,)), HI)
        q_ref[:, at] = q
        ro[...] = ro[...] - dot(q, panel, ((1,), (0,)), HI)
        af[...] = af[...] - dot(panel, panel, ((0,), (0,)), HI)
        return carry

    lax.fori_loop(0, blocks, eliminate, 0)

    wait_recv(*updates)
    for k in range(1, nb):
        cross(k).wait_send()
    for phase in (grads, bases, squares, shares, stats, moments, updates):
        wait_send(*phase)


def ceil_to(value, step):
    return -(-value // step) * step


def local(n, nb, gradient, first_moment, second_moment, statistic, eigenbasis):
    rows, ff = gradient.shape[1:]
    bk = rows * n
    cols = ff // n
    rp = ceil_to(rows, 16)
    rf_rows = ceil_to(rows, 8)
    kp = ceil_to(bk, NB)
    split = cols % 128 != 0

    def wide(x):
        x = jnp.pad(x[0], ((0, rp - rows), (0, 0)))
        if split:
            x = jnp.swapaxes(x.reshape(rp, n, cols), 0, 1)
        return x

    def narrow(x):
        if split:
            x = jnp.swapaxes(x, 0, 1).reshape(rp, ff)
        return x[None, :rows]

    def square(x):
        return jnp.pad(x[0], ((0, rf_rows - rows), (0, kp - bk)))

    pick = np.zeros((kp, n * rp), np.float32)
    at = np.arange(bk)
    pick[at, (at // rows) * rp + at % rows] = 1.0
    big = (n, rp, cols) if split else (rp, ff)
    vmem = pl.BlockSpec(memory_space=pltpu.VMEM)
    dma = pltpu.SemaphoreType.DMA
    upd, nf, ns, nst, q = pl.pallas_call(
        functools.partial(kernel, n, nb, nb * bk * ff, cols, bk, split),
        out_shape=(
            jax.ShapeDtypeStruct(big, BF16),
            jax.ShapeDtypeStruct(big, BF16),
            jax.ShapeDtypeStruct((bk, cols), BF16),
            jax.ShapeDtypeStruct((rf_rows, kp), F32),
            jax.ShapeDtypeStruct((rf_rows, kp), F32),
        ),
        in_specs=[vmem] * 6,
        out_specs=(vmem,) * 5,
        scratch_shapes=[
            pltpu.VMEM((n, rp, cols), BF16),
            pltpu.VMEM((n, rp, cols), BF16),
            pltpu.VMEM((n, rp, cols), BF16),
            pltpu.VMEM((bk, cols), F32),
            pltpu.VMEM((n, rf_rows, kp), F32),
            pltpu.VMEM((n, rp, kp), BF16),
            pltpu.VMEM((n, rf_rows, kp), F32),
            pltpu.VMEM((n, rf_rows, kp), F32),
            pltpu.VMEM((n, rf_rows, kp), F32),
            pltpu.VMEM((kp, cols), BF16),
            pltpu.VMEM((kp, kp), F32),
            pltpu.VMEM((kp, kp), F32),
            pltpu.VMEM((rf_rows, kp), F32),
            pltpu.VMEM((n + 1, 8, 128), F32),
            pltpu.VMEM((nb + 1, 8, 128), F32),
            pltpu.VMEM((NB, NB), F32),
        ]
        + [dma((n,))] * 14
        + [dma((nb,))] * 2
        + [dma((3,))],
        compiler_params=pltpu.CompilerParams(
            collective_id=0, has_side_effects=True, vmem_limit_bytes=56 * 1024 * 1024
        ),
    )(
        wide(gradient),
        wide(first_moment),
        second_moment[0],
        square(statistic),
        square(eigenbasis),
        jnp.asarray(pick, BF16),
    )
    return (narrow(upd), narrow(nf), ns[None], nst[None, :rows, :bk], q[None, :rows, :bk])


def solution(mesh):
    n, nb = mesh.shape["fsdp"], mesh.shape["basis"]
    rows = P("basis", "fsdp", None)
    columns = P("basis", None, "fsdp")
    return jax.shard_map(
        functools.partial(local, n, nb),
        mesh=mesh,
        in_specs=(rows, rows, columns, rows, rows),
        out_specs=(rows, rows, columns, rows, rows),
        check_vma=False,
    )
```

time: 829 us -> 290 us (0.35); the launches traced: 815 us -> 286 us
  other arithmetic: 374 us -> 0 us
  Pallas kernels: 0 us -> 272 us
  local copies, waits for them, and re-layouts: 174 us -> 13.5 us
  waiting for transfers between devices: 89.8 us -> 0 us
  blocking collectives: 89.7 us -> 0 us
  starting transfers between devices: 43.9 us -> 0 us
  matrix products: 22.9 us -> 0 us
  between operations: 19.6 us -> 0.67 us
    pallas_call x0 -> x1, Pallas kernels: none -> 272 us  [local(): pl.pallas_call(functools.partial(kernel, n, nb, nb * bk * ff, cols, bk, s...]
    unnamed x4 -> x0, other arithmetic: 214 us -> none
    another operation x25 -> x0, other arithmetic: 153 us -> none  [the longest x18 103 us: local(): factor = jnp.linalg.cholesky(gram_matrix)]
    unnamed x44 -> x13, local copies, waits for them, and re-layouts: 108 us -> 4.34 us
    psum x1 -> x0, waiting for transfers between devices: 86.9 us -> none  [local(): lax.psum(lead_dot(refreshed, refreshed, lax.Precision.HIGHEST), 'fsdp')]
    all_to_all x10 -> x0, local copies, waits for them, and re-layouts: 49.6 us -> none  [the longest x3 18.3 us: local(): lax.all_to_all(gradient, 'fsdp', split_axis=2, concat_axis=1, tiled=True)]
    unnamed x1 -> x0, blocking collectives: 49.6 us -> none
    psum x1 -> x0, blocking collectives: 40.2 us -> none  [local(): total_squares = lax.psum(local_squares, ('fsdp', 'basis'))]
  transfers between devices with their start and end apart: 9 -> 0, of which waited for: 2 -> 0; matrix products, arithmetic and copies ran while one was open for 57% -> 0% of each run, Pallas kernels for 0% -> 0%
where the time goes in v1:
time: 290 us; the launch traced here: 286 us
  Pallas kernels  272 us (94%)
  local copies, waits for them, and re-layouts  13.5 us (5%)
    pallas_call x1, Pallas kernels, local(): pl.pallas_call(functools.partial(kernel, n, nb, nb * bk * ff, cols, bk, s...  272 us

profile of v1, /device:TPU:26, one launch (start us, length us, event | category | flops | bytes accessed | tf_op | source)
XLA Modules:
  0.0 286.0 jit_solution(3158032441158273110)
XLA Ops:
  0.6 0.9 copy.18
  1.5 0.6 pad.16.st_ref
  2.2 0.9 copy.17
  3.1 0.6 pad.17.eb_ref
  3.7 0.0 copy-start
  3.7 2.8 pad.14.g_ref
  6.6 0.0 copy-done
  6.6 1.3 pad.15.m_ref
  7.9 271.8 %shard_map.101 = (bf16[48,18432]{1,0:T(8,128)(2,1)}, bf16[48,18432]{1,0:T(8,128)(2,1)}, bf16[576,1152]{1,0:T(8,128)(2,1)}, f32[40,640]{1,0:T(8,128)}, f32[40,640]{1,0:T(8,128)}) custom-call(bf16[48,18432]{1,0:T(8,128)(2,1)} %pad.14.g_ref, bf16[48,18432]{1,0:T(8,128)(2,1)} %pad.15.m_ref, bf16[576,1152]{1,0:T(8,128)(2,1)} %bitcast.21, f32[40,640]{1,0:T(8,128)} %pad.16.st_ref, ...), custom_call_target="tpu_custom_call" | custom-call | tf_op jit(solution)/shard_map/pallas_call | solution.py:335
  279.7 0.0 copy-start.2
  279.7 0.0 copy-start.3
  279.7 0.0 copy-start.1
  279.7 3.7 %slice_bitcast_fusion = (bf16[1,36,18432]{2,1,0:T(8,128)(2,1)}, bf16[1,36,18432]{2,1,0:T(8,128)(2,1)}) fusion(bf16[48,18432]{1,0:T(8,128)(2,1)} %get-tuple-element.11, bf16[48,18432]{1,0:T(8,128)(2,1)} %get-tuple-element.10), kind=kLoop, calls=%fused_computation | loop fusion | bytes 5308416 | tf_op jit(solution)/shard_map/broadcast_in_dim | solution.py:324
  283.4 0.0 copy-done.2
  283.4 0.0 copy-done.3
  283.5 0.7 copy.12
  284.2 0.7 copy.11
  284.9 0.0 copy-done.1
  284.9 1.1 copy.20
  (1 shorter events, 0.0 us)
Async XLA Ops:
  3.7 2.8 copy-start
  279.7 3.7 %copy-start.2 = (f32[40,640]{1,0:T(8,128)S(1)}, f32[40,640]{1,0:T(8,128)}, u32[]{:S(2)}) copy-start(f32[40,640]{1,0:T(8,128)} %get-tuple-element.13) | copy-start | bytes 307204
  279.7 3.7 %copy-start.3 = (f32[40,640]{1,0:T(8,128)S(1)}, f32[40,640]{1,0:T(8,128)}, u32[]{:S(2)}) copy-start(f32[40,640]{1,0:T(8,128)} %get-tuple-element.14) | copy-start | bytes 307204
  279.7 5.2 %copy-start.1 = (bf16[576,1152]{1,0:T(8,128)(2,1)S(1)}, bf16[576,1152]{1,0:T(8,128)(2,1)}, u32[]{:S(2)}) copy-start(bf16[576,1152]{1,0:T(8,128)(2,1)} %get-tuple-element.12) | copy-start | bytes 3981316

commit v2 on v1

--- a/solution.py
+++ b/solution.py
@@ -25,17 +25,18 @@
     )
 
 
-def inverse_factor(tiles):
+def inverse_factor(tiles, steps):
     lane = lax.broadcasted_iota(jnp.int32, (8, NB), 1)
     row = lax.broadcasted_iota(jnp.int32, (8, NB), 0)
     count = NB // 8
-    for j in range(NB):
+    active = -(-steps // 8)
+    for j in range(steps):
         home, sub = divmod(j, 8)
         pivot_row = tiles[home][sub : sub + 1, :]
         inverse = 1.0 / pivot_row[:, j : j + 1]
         at_j = lane == j
         scaled = jnp.where(at_j[:1], 1.0, pivot_row) * inverse
-        for t in range(home, count):
+        for t in range(home, active):
             column = tiles[t][:, j : j + 1]
             updated = jnp.where(at_j, 0.0, tiles[t]) - column * scaled
             tiles[t] = jnp.where(row > sub, updated, tiles[t]) if t == home else updated
@@ -99,12 +100,65 @@
             ).wait_send()
         peers(one)
 
+    plane = 4 if n % 4 == 0 else 1
+    mine = lax.rem(me, plane)
+    base = me - mine
+
+    def gather_copy(source, target, s_sem, r_sem, slot, d, s_at):
+        return pltpu.make_async_remote_copy(
+            src_ref=source, dst_ref=target(slot), send_sem=s_sem.at[s_at],
+            recv_sem=r_sem.at[slot], device_id={"fsdp": d}, device_id_type=MESH,
+        )
+
+    def across(fn):
+        def body(k, carry):
+            fn(lax.rem(me + plane * k, n))
+            return carry
+        lax.fori_loop(1, n // plane, body, 0)
+
+    def inside(fn):
+        for k in range(1, plane):
+            fn(base + lax.rem(mine + k, plane))
+
+    def gather_start(source, target, s_sem, r_sem):
+        def one(d):
+            gather_copy(source, target, s_sem, r_sem, me, d, d).start()
+        across(one)
+        inside(one)
+
+    def gather_forward(source, target, s_sem, r_sem):
+        def one(z):
+            gather_copy(source, target, s_sem, r_sem, z, z, z).wait_recv()
+
+            def on(p):
+                gather_copy(target(z), target, s_sem, r_sem, z, p, z - mine + p - base).start()
+
+            inside(on)
+        across(one)
+
+    def gather_finish(source, target, s_sem, r_sem):
+        def near(p):
+            gather_copy(source, target, s_sem, r_sem, p, p, p).wait_recv()
+
+            def far(z):
+                slot = z - mine + p - base
+                gather_copy(source, target, s_sem, r_sem, slot, p, slot).wait_recv()
+
+            across(far)
+
+        inside(near)
+
+    def gather_sent(source, target, s_sem, r_sem):
+        def one(d):
+            gather_copy(source, target, s_sem, r_sem, d, d, d).wait_send()
+        peers(one)
+
     grads = (lambda d: chunk(g_ref, d), lambda s: gs.at[s], g_s, g_r)
     moments = (lambda d: chunk(m_ref, d), lambda s: ms.at[s], m_s, m_r)
     updates = (lambda d: us.at[d], lambda s: chunk(upd_ref, s), u_s, u_r)
-    bases = (lambda d: eb_ref, lambda s: bs.at[s], b_s, b_r)
+    bases = (eb_ref, lambda s: bs.at[s], b_s, b_r)
     shares = (lambda d: covs.at[d], lambda s: rs.at[s], c_s, c_r)
-    stats = (lambda d: nst_ref, lambda s: ss.at[s], a_s, a_r)
+    stats = (nst_ref, lambda s: ss.at[s], a_s, a_r)
     squares = (lambda d: sums_a.at[n], lambda s: sums_a.at[s], x_s, x_r)
 
     barrier = pltpu.get_barrier_semaphore()
@@ -120,7 +174,7 @@
     pl.semaphore_wait(barrier, n - 1 + nb - 1)
 
     send(*grads)
-    send(*bases)
+    gather_start(*bases)
     own = [
         pltpu.make_async_copy(chunk(g_ref, me), gs.at[me], own_sem.at[0]),
         pltpu.make_async_copy(chunk(m_ref, me), ms.at[me], own_sem.at[1]),
@@ -169,6 +223,7 @@
 
     lax.fori_loop(0, n, share, 0)
     send(*shares)
+    gather_forward(*bases)
 
     for k in range(1, nb):
         cross_recv(k).wait_recv()
@@ -184,7 +239,7 @@
 
     lax.fori_loop(0, n, first, 0)
 
-    wait_recv(*bases)
+    gather_finish(*bases)
 
     def narrow(s, carry):
         v = bs[s]
@@ -220,10 +275,11 @@
 
     cov = lax.fori_loop(0, n, add_share, jnp.zeros((rf_rows, kp), F32)) / total
     nst_ref[...] = beta_second * st_ref[...] + (1.0 - beta_second) * clip * clip * cov
-    send(*stats)
+    gather_start(*stats)
+    ss[me] = nst_ref[...]
+    gather_forward(*stats)
+    gather_finish(*stats)
     send(*moments)
-    ss[me] = nst_ref[...]
-    wait_recv(*stats)
 
     def refresh(i, carry):
         at = pl.ds(pl.multiple_of(i * NB, NB), NB)
@@ -273,30 +329,38 @@
 
     blocks = kp // NB
 
-    def eliminate(b, carry):
-        @pl.when(b == blocks // 2)
-        def _():
-            precondition()
-
+    def eliminate(b, steps):
         at = pl.ds(pl.multiple_of(b * NB, NB), NB)
         tiles = [
             af[pl.ds(pl.multiple_of(b * NB + 8 * t, 8), 8), at] for t in range(NB // 8)
         ]
-        lin[...] = inverse_factor(tiles)
+        lin[...] = inverse_factor(tiles, steps)
         panel = dot(lin[...], af[at, :], ((1,), (0,)), HI)
         q = dot(ro[:, at], lin[...], ((1,), (1,)), HI)
         q_ref[:, at] = q
         ro[...] = ro[...] - dot(q, panel, ((1,), (0,)), HI)
-        af[...] = af[...] - dot(panel, panel, ((0,), (0,)), HI)
-        return carry
-
-    lax.fori_loop(0, blocks, eliminate, 0)
+        if steps == NB:
+            af[...] = af[...] - dot(panel, panel, ((0,), (0,)), HI)
+
+    def whole_block(b, carry):
+        @pl.when(b == blocks // 2)
+        def _():
+            precondition()
+
+        eliminate(b, NB)
+        return carry
+
+    last = bk - (blocks - 1) * NB
+    lax.fori_loop(0, blocks - 1, whole_block, 0)
+    eliminate(blocks - 1, last)
 
     wait_recv(*updates)
     for k in range(1, nb):
         cross(k).wait_send()
-    for phase in (grads, bases, squares, shares, stats, moments, updates):
+    for phase in (grads, squares, shares, moments, updates):
         wait_send(*phase)
+    gather_sent(*bases)
+    gather_sent(*stats)
 
 
 def ceil_to(value, step):

time: 290 us -> 236 us (0.81)
  the two profiles are of different devices: /device:TPU:26 before, /device:TPU:0 now
where the time goes in v2:
time: 236 us
  Pallas kernels  221 us (94%)
  local copies, waits for them, and re-layouts  13.5 us (6%)
    pallas_call x1, Pallas kernels, local(): pl.pallas_call(functools.partial(kernel, n, nb, nb * bk * ff, cols, bk, s...  221 us

profile of v2, /device:TPU:0, one launch (start us, length us, event | category | flops | bytes accessed | tf_op | source)
XLA Modules:
  0.0 235.7 jit_solution(9961448090191340135)
XLA Ops:
  0.6 0.9 copy.18
  1.5 0.6 pad.16.st_ref
  2.2 0.9 copy.17
  3.1 0.6 pad.17.eb_ref
  3.7 0.0 copy-start
  3.7 2.8 %pad.14.g_ref = bf16[48,18432]{1,0:T(8,128)(2,1)} pad(bf16[36,18432]{1,0:T(8,128)(2,1)} %bitcast.18, bf16[]{:T(256)} %constant.5.clone.1), padding=0_12x0_0 | pad | bytes 3096578 | tf_op jit(solution)/shard_map/jit(_pad)/pad | solution.py:380
  6.6 0.0 copy-done
  6.6 1.3 pad.15.m_ref
  7.9 221.5 %shard_map.101 = (bf16[48,18432]{1,0:T(8,128)(2,1)}, bf16[48,18432]{1,0:T(8,128)(2,1)}, bf16[576,1152]{1,0:T(8,128)(2,1)}, f32[40,640]{1,0:T(8,128)}, f32[40,640]{1,0:T(8,128)}) custom-call(bf16[48,18432]{1,0:T(8,128)(2,1)} %pad.14.g_ref, bf16[48,18432]{1,0:T(8,128)(2,1)} %pad.15.m_ref, bf16[576,1152]{1,0:T(8,128)(2,1)} %bitcast.21, f32[40,640]{1,0:T(8,128)} %pad.16.st_ref, ...), custom_call_target="tpu_custom_call" | custom-call | tf_op jit(solution)/shard_map/pallas_call | solution.py:399
  229.4 0.0 copy-start.2
  229.4 0.0 copy-start.3
  229.4 0.0 copy-start.1
  229.4 3.7 %slice_bitcast_fusion = (bf16[1,36,18432]{2,1,0:T(8,128)(2,1)}, bf16[1,36,18432]{2,1,0:T(8,128)(2,1)}) fusion(bf16[48,18432]{1,0:T(8,128)(2,1)} %get-tuple-element.11, bf16[48,18432]{1,0:T(8,128)(2,1)} %get-tuple-element.10), kind=kLoop, calls=%fused_computation | loop fusion | bytes 5308416 | tf_op jit(solution)/shard_map/broadcast_in_dim | solution.py:388
  233.1 0.0 copy-done.2
  233.1 0.0 copy-done.3
  233.2 0.7 copy.12
  233.9 0.7 copy.11
  234.6 0.0 copy-done.1
  234.6 1.1 copy.20
  (1 shorter events, 0.0 us)
Async XLA Ops:
  3.7 2.8 %copy-start = (bf16[1,36,18432]{2,1,0:T(8,128)(2,1)S(1)}, bf16[1,36,18432]{2,1,0:T(8,128)(2,1)}, u32[]{:S(2)}) copy-start(bf16[1,36,18432]{2,1,0:T(8,128)(2,1)} %param.7) | copy-start | bytes 3981316
  229.4 3.7 %copy-start.2 = (f32[40,640]{1,0:T(8,128)S(1)}, f32[40,640]{1,0:T(8,128)}, u32[]{:S(2)}) copy-start(f32[40,640]{1,0:T(8,128)} %get-tuple-element.13) | copy-start | bytes 307204
  229.4 3.7 %copy-start.3 = (f32[40,640]{1,0:T(8,128)S(1)}, f32[40,640]{1,0:T(8,128)}, u32[]{:S(2)}) copy-start(f32[40,640]{1,0:T(8,128)} %get-tuple-element.14) | copy-start | bytes 307204
  229.4 5.2 %copy-start.1 = (bf16[576,1152]{1,0:T(8,128)(2,1)S(1)}, bf16[576,1152]{1,0:T(8,128)(2,1)}, u32[]{:S(2)}) copy-start(bf16[576,1152]{1,0:T(8,128)(2,1)} %get-tuple-element.12) | copy-start | bytes 3981316

commit v3 on v2

--- a/solution.py
+++ b/solution.py
@@ -30,16 +30,33 @@
     row = lax.broadcasted_iota(jnp.int32, (8, NB), 0)
     count = NB // 8
     active = -(-steps // 8)
-    for j in range(steps):
+    for j in range(0, steps, 2):
         home, sub = divmod(j, 8)
-        pivot_row = tiles[home][sub : sub + 1, :]
-        inverse = 1.0 / pivot_row[:, j : j + 1]
-        at_j = lane == j
-        scaled = jnp.where(at_j[:1], 1.0, pivot_row) * inverse
+        here, after = lane == j, lane == j + 1
+        one = tiles[home][sub : sub + 1, :]
+        two = tiles[home][sub + 1 : sub + 2, :]
+        cross = two[:, j : j + 1]
+        inverse = 1.0 / one[:, j : j + 1]
+        ratio = cross * inverse
+        inverse_two = 1.0 / (two[:, j + 1 : j + 2] - cross * ratio)
+        lead = jnp.where(here[:1], 1.0, jnp.where(after[:1], 0.0, one))
+        trail = jnp.where(
+            after[:1], 1.0, jnp.where(here[:1], 0.0, two) - ratio * lead
+        )
+        scaled_two = trail * inverse_two
+        scaled_one = lead * inverse - ratio * scaled_two
+        kept = jnp.where(after[:1], two - ratio * one, trail)
         for t in range(home, active):
             column = tiles[t][:, j : j + 1]
-            updated = jnp.where(at_j, 0.0, tiles[t]) - column * scaled
-            tiles[t] = jnp.where(row > sub, updated, tiles[t]) if t == home else updated
+            column_two = tiles[t][:, j + 1 : j + 2]
+            updated = (
+                jnp.where(here | after, 0.0, tiles[t])
+                - column * scaled_one - column_two * scaled_two
+            )
+            if t == home:
+                updated = jnp.where(row > sub + 1, updated, tiles[t])
+                updated = jnp.where(row == sub + 1, kept, updated)
+            tiles[t] = updated
     out = []
     for t in range(count):
         on_diag = lane == row + 8 * t
@@ -53,7 +70,7 @@
     n, nb, entries, cols, bk, split,
     g_ref, m_ref, v_ref, st_ref, eb_ref, pm_ref,
     upd_ref, nf_ref, ns_ref, nst_ref, q_ref,
-    gs, ms, us, gr, bs, bb, covs, rs, ss, gc, rf, af, ro, sums_a, sums_b, lin,
+    gs, ms, us, gr, bs, bb, covs, rs, ss, gc, rf, af, ro, sums_a, sums_b, lin, rt, f_s, f_r,
     g_s, g_r, m_s, m_r, u_s, u_r, b_s, b_r, c_s, c_r, a_s, a_r, x_s, x_r, y_s, y_r, own_sem,
 ):
     me = lax.axis_index("fsdp")
@@ -157,7 +174,6 @@
     moments = (lambda d: chunk(m_ref, d), lambda s: ms.at[s], m_s, m_r)
     updates = (lambda d: us.at[d], lambda s: chunk(upd_ref, s), u_s, u_r)
     bases = (eb_ref, lambda s: bs.at[s], b_s, b_r)
-    shares = (lambda d: covs.at[d], lambda s: rs.at[s], c_s, c_r)
     stats = (nst_ref, lambda s: ss.at[s], a_s, a_r)
     squares = (lambda d: sums_a.at[n], lambda s: sums_a.at[s], x_s, x_r)
 
@@ -222,8 +238,31 @@
         return carry
 
     lax.fori_loop(0, n, share, 0)
-    send(*shares)
+    per = n // plane
+
+    def near_copy(p, k, slot, sem):
+        return pltpu.make_async_remote_copy(
+            src_ref=covs.at[slot], dst_ref=rs.at[sem], send_sem=c_s.at[slot],
+            recv_sem=c_r.at[sem], device_id={"fsdp": p}, device_id_type=MESH,
+        )
+
+    def each_near(fn):
+        def on(p):
+            def body(k, carry):
+                fn(p, k)
+                return carry
+            lax.fori_loop(0, per, body, 0)
+        inside(on)
+
+    def far_copy(z, slot):
+        return pltpu.make_async_remote_copy(
+            src_ref=covs.at[z], dst_ref=rt.at[slot], send_sem=f_s.at[z],
+            recv_sem=f_r.at[slot], device_id={"fsdp": z}, device_id_type=MESH,
+        )
+
+    each_near(lambda p, k: near_copy(p, k, k * plane + p - base, mine * per + k).start())
     gather_forward(*bases)
+    send(*moments)
 
     for k in range(1, nb):
         cross_recv(k).wait_recv()
@@ -267,19 +306,35 @@
 
     lax.fori_loop(0, cols // width, rotate, 0)
 
-    wait_recv(*shares)
-    rs[me] = covs[me]
-
-    def add_share(s, acc):
-        return acc + rs[s]
-
-    cov = lax.fori_loop(0, n, add_share, jnp.zeros((rf_rows, kp), F32)) / total
+    each_near(
+        lambda p, k: near_copy(p, k, k * plane + p - base, (p - base) * per + k).wait_recv()
+    )
+    level = base // plane
+
+    def plane_sum(z):
+        k = (z - mine) // plane
+        acc = covs[z]
+        for step in range(1, plane):
+            acc = acc + rs[lax.rem(mine + step, plane) * per + k]
+        return acc
+
+    def pass_on(z):
+        covs[z] = plane_sum(z)
+        far_copy(z, level).start()
+
+    across(pass_on)
+    rt[level] = plane_sum(me)
+    across(lambda z: far_copy(z, (z - mine) // plane).wait_recv())
+
+    def add_share(k, acc):
+        return acc + rt[k]
+
+    cov = lax.fori_loop(0, per, add_share, jnp.zeros((rf_rows, kp), F32)) / total
     nst_ref[...] = beta_second * st_ref[...] + (1.0 - beta_second) * clip * clip * cov
     gather_start(*stats)
     ss[me] = nst_ref[...]
     gather_forward(*stats)
     gather_finish(*stats)
-    send(*moments)
 
     def refresh(i, carry):
         at = pl.ds(pl.multiple_of(i * NB, NB), NB)
@@ -343,7 +398,7 @@
             af[...] = af[...] - dot(panel, panel, ((0,), (0,)), HI)
 
     def whole_block(b, carry):
-        @pl.when(b == blocks // 2)
+        @pl.when(b == 1)
         def _():
             precondition()
 
@@ -357,8 +412,10 @@
     wait_recv(*updates)
     for k in range(1, nb):
         cross(k).wait_send()
-    for phase in (grads, squares, shares, moments, updates):
+    for phase in (grads, squares, moments, updates):
         wait_send(*phase)
+    each_near(lambda p, k: near_copy(p, k, k * plane + p - base, mine * per + k).wait_send())
+    across(lambda z: far_copy(z, level).wait_send())
     gather_sent(*bases)
     gather_sent(*stats)
 
@@ -424,8 +481,9 @@
             pltpu.VMEM((n + 1, 8, 128), F32),
             pltpu.VMEM((nb + 1, 8, 128), F32),
             pltpu.VMEM((NB, NB), F32),
+            pltpu.VMEM((n, rf_rows, kp), F32),
         ]
-        + [dma((n,))] * 14
+        + [dma((n,))] * 16
         + [dma((nb,))] * 2
         + [dma((3,))],
         compiler_params=pltpu.CompilerParams(

time: 236 us -> 252 us (1.068)
  the two profiles are of different devices: /device:TPU:0 before, /device:TPU:26 now
where the time goes in v3:
time: 252 us
  Pallas kernels  238 us (94%)
  local copies, waits for them, and re-layouts  13.5 us (5%)
    pallas_call x1, Pallas kernels, local(): pl.pallas_call(functools.partial(kernel, n, nb, nb * bk * ff, cols, bk, s...  238 us

profile of v3, /device:TPU:26, one launch (start us, length us, event | category | flops | bytes accessed | tf_op | source)
XLA Modules:
  0.0 251.8 jit_solution(3826237399075856532)
XLA Ops:
  0.6 0.9 copy.18
  1.5 0.6 pad.16.st_ref
  2.2 0.9 copy.17
  3.1 0.6 pad.17.eb_ref
  3.7 0.0 copy-start
  3.7 2.8 %pad.14.g_ref = bf16[48,18432]{1,0:T(8,128)(2,1)} pad(bf16[36,18432]{1,0:T(8,128)(2,1)} %bitcast.18, bf16[]{:T(256)} %constant.5.clone.1), padding=0_12x0_0 | pad | bytes 3096578 | tf_op jit(solution)/shard_map/jit(_pad)/pad | solution.py:437
  6.6 0.0 copy-done
  6.6 1.3 pad.15.m_ref
  7.9 237.6 %shard_map.101 = (bf16[48,18432]{1,0:T(8,128)(2,1)}, bf16[48,18432]{1,0:T(8,128)(2,1)}, bf16[576,1152]{1,0:T(8,128)(2,1)}, f32[40,640]{1,0:T(8,128)}, f32[40,640]{1,0:T(8,128)}) custom-call(bf16[48,18432]{1,0:T(8,128)(2,1)} %pad.14.g_ref, bf16[48,18432]{1,0:T(8,128)(2,1)} %pad.15.m_ref, bf16[576,1152]{1,0:T(8,128)(2,1)} %bitcast.21, f32[40,640]{1,0:T(8,128)} %pad.16.st_ref, ...), custom_call_target="tpu_custom_call" | custom-call | tf_op jit(solution)/shard_map/pallas_call | solution.py:456
  245.5 0.0 copy-start.2
  245.5 0.0 copy-start.3
  245.5 0.0 copy-start.1
  245.5 3.7 %slice_bitcast_fusion = (bf16[1,36,18432]{2,1,0:T(8,128)(2,1)}, bf16[1,36,18432]{2,1,0:T(8,128)(2,1)}) fusion(bf16[48,18432]{1,0:T(8,128)(2,1)} %get-tuple-element.11, bf16[48,18432]{1,0:T(8,128)(2,1)} %get-tuple-element.10), kind=kLoop, calls=%fused_computation | loop fusion | bytes 5308416 | tf_op jit(solution)/shard_map/broadcast_in_dim | solution.py:445
  249.2 0.0 copy-done.2
  249.2 0.0 copy-done.3
  249.2 0.7 copy.12
  250.0 0.7 copy.11
  250.7 0.0 copy-done.1
  250.7 1.1 copy.20
  (1 shorter events, 0.0 us)
Async XLA Ops:
  3.7 2.8 %copy-start = (bf16[1,36,18432]{2,1,0:T(8,128)(2,1)S(1)}, bf16[1,36,18432]{2,1,0:T(8,128)(2,1)}, u32[]{:S(2)}) copy-start(bf16[1,36,18432]{2,1,0:T(8,128)(2,1)} %param.7) | copy-start | bytes 3981316
  245.5 3.7 %copy-start.2 = (f32[40,640]{1,0:T(8,128)S(1)}, f32[40,640]{1,0:T(8,128)}, u32[]{:S(2)}) copy-start(f32[40,640]{1,0:T(8,128)} %get-tuple-element.13) | copy-start | bytes 307204
  245.5 3.7 %copy-start.3 = (f32[40,640]{1,0:T(8,128)S(1)}, f32[40,640]{1,0:T(8,128)}, u32[]{:S(2)}) copy-start(f32[40,640]{1,0:T(8,128)} %get-tuple-element.14) | copy-start | bytes 307204
  245.5 5.2 %copy-start.1 = (bf16[576,1152]{1,0:T(8,128)(2,1)S(1)}, bf16[576,1152]{1,0:T(8,128)(2,1)}, u32[]{:S(2)}) copy-start(bf16[576,1152]{1,0:T(8,128)(2,1)} %get-tuple-element.12) | copy-start | bytes 3981316

commit v4 on v3

--- a/solution.py
+++ b/solution.py
@@ -262,7 +262,6 @@
 
     each_near(lambda p, k: near_copy(p, k, k * plane + p - base, mine * per + k).start())
     gather_forward(*bases)
-    send(*moments)
 
     for k in range(1, nb):
         cross_recv(k).wait_recv()
@@ -335,6 +334,7 @@
     ss[me] = nst_ref[...]
     gather_forward(*stats)
     gather_finish(*stats)
+    send(*moments)
 
     def refresh(i, carry):
         at = pl.ds(pl.multiple_of(i * NB, NB), NB)
@@ -398,7 +398,7 @@
             af[...] = af[...] - dot(panel, panel, ((0,), (0,)), HI)
 
     def whole_block(b, carry):
-        @pl.when(b == 1)
+        @pl.when(b == blocks // 2)
         def _():
             precondition()
 

time: 252 us -> 248 us (0.984); the launches traced: 252 us -> 244 us
  Pallas kernels: 238 us -> 230 us
    pallas_call x1, Pallas kernels: 238 us -> 230 us  [local(): pl.pallas_call(functools.partial(kernel, n, nb, nb * bk * ff, cols, bk, s...]
where the time goes in v4:
time: 248 us; the launch traced here: 244 us
  Pallas kernels  230 us (93%)
  local copies, waits for them, and re-layouts  13.5 us (5%)
    pallas_call x1, Pallas kernels, local(): pl.pallas_call(functools.partial(kernel, n, nb, nb * bk * ff, cols, bk, s...  230 us

profile of v4, /device:TPU:26, one launch (start us, length us, event | category | flops | bytes accessed | tf_op | source)
XLA Modules:
  0.0 244.0 jit_solution(11447438173383879888)
XLA Ops:
  0.6 0.9 copy.18
  1.5 0.6 pad.16.st_ref
  2.2 0.9 copy.17
  3.1 0.6 pad.17.eb_ref
  3.7 0.0 copy-start
  3.7 2.8 %pad.14.g_ref = bf16[48,18432]{1,0:T(8,128)(2,1)} pad(bf16[36,18432]{1,0:T(8,128)(2,1)} %bitcast.18, bf16[]{:T(256)} %constant.5.clone.1), padding=0_12x0_0 | pad | bytes 3096578 | tf_op jit(solution)/shard_map/jit(_pad)/pad | solution.py:437
  6.6 0.0 copy-done
  6.6 1.3 pad.15.m_ref
  7.9 229.8 %shard_map.101 = (bf16[48,18432]{1,0:T(8,128)(2,1)}, bf16[48,18432]{1,0:T(8,128)(2,1)}, bf16[576,1152]{1,0:T(8,128)(2,1)}, f32[40,640]{1,0:T(8,128)}, f32[40,640]{1,0:T(8,128)}) custom-call(bf16[48,18432]{1,0:T(8,128)(2,1)} %pad.14.g_ref, bf16[48,18432]{1,0:T(8,128)(2,1)} %pad.15.m_ref, bf16[576,1152]{1,0:T(8,128)(2,1)} %bitcast.21, f32[40,640]{1,0:T(8,128)} %pad.16.st_ref, ...), custom_call_target="tpu_custom_call" | custom-call | tf_op jit(solution)/shard_map/pallas_call | solution.py:456
  237.7 0.0 copy-start.2
  237.7 0.0 copy-start.3
  237.7 0.0 copy-start.1
  237.7 3.7 %slice_bitcast_fusion = (bf16[1,36,18432]{2,1,0:T(8,128)(2,1)}, bf16[1,36,18432]{2,1,0:T(8,128)(2,1)}) fusion(bf16[48,18432]{1,0:T(8,128)(2,1)} %get-tuple-element.11, bf16[48,18432]{1,0:T(8,128)(2,1)} %get-tuple-element.10), kind=kLoop, calls=%fused_computation | loop fusion | bytes 5308416 | tf_op jit(solution)/shard_map/broadcast_in_dim | solution.py:445
  241.4 0.0 copy-done.2
  241.4 0.0 copy-done.3
  241.4 0.7 copy.12
  242.2 0.7 copy.11
  242.9 0.0 copy-done.1
  242.9 1.1 copy.20
  (1 shorter events, 0.0 us)
Async XLA Ops:
  3.7 2.8 %copy-start = (bf16[1,36,18432]{2,1,0:T(8,128)(2,1)S(1)}, bf16[1,36,18432]{2,1,0:T(8,128)(2,1)}, u32[]{:S(2)}) copy-start(bf16[1,36,18432]{2,1,0:T(8,128)(2,1)} %param.7) | copy-start | bytes 3981316
  237.7 3.7 %copy-start.2 = (f32[40,640]{1,0:T(8,128)S(1)}, f32[40,640]{1,0:T(8,128)}, u32[]{:S(2)}) copy-start(f32[40,640]{1,0:T(8,128)} %get-tuple-element.13) | copy-start | bytes 307204
  237.7 3.7 %copy-start.3 = (f32[40,640]{1,0:T(8,128)S(1)}, f32[40,640]{1,0:T(8,128)}, u32[]{:S(2)}) copy-start(f32[40,640]{1,0:T(8,128)} %get-tuple-element.14) | copy-start | bytes 307204
  237.7 5.2 %copy-start.1 = (bf16[576,1152]{1,0:T(8,128)(2,1)S(1)}, bf16[576,1152]{1,0:T(8,128)(2,1)}, u32[]{:S(2)}) copy-start(bf16[576,1152]{1,0:T(8,128)(2,1)} %get-tuple-element.12) | copy-start | bytes 3981316
